TPU v7x, 256 devices: a whole 4x4x8 slice. The times are simulated.
256 devices in a mesh: layer: 64 (over x, z, core), col: 4 (over y).
Axes of the slice: x: 4, y: 4, z: 8, core: 2. Of those that a mesh axis runs over, the one named last changes fastest.
Arguments:
- l_panels: bfloat16 [64, 2048, 2048], P('layer', None, 'col'), may hold values from -6 to 6
- u_panels: bfloat16 [64, 2048, 2048], P('layer', None, 'col'), may hold values from -0.125 to 0.125
- l_masks: int32 [64, 8, 8], P('layer'), may hold values 0 or 1
- u_masks: int32 [64, 8, 8], P('layer'), may hold values 0 or 1
- ancestor_tiles: int32 [8, 8], replicated, may hold values 0 or 1
- initial: float32 [2048, 2048], P('layer', 'col'), may hold values from -6 to 6
Outputs:
- schur: float32 [2048, 2048], P('layer', 'col')
All inputs are finite; a program needn't handle non-finite values. No bound on the sum of `l_masks` or of `u_masks` on one device may be relied on, other than what follows from the above.
Results may differ from a plain program's by a relative error of at most 0.0003.
Values may be sent and summed in bfloat16 or wider, within the bound.
A program may use at most 64 MiB of HBM per device.

v0:
```python
import jax
import jax.numpy as jnp
from jax import lax
from jax.sharding import PartitionSpec as P

TILE = 256


def expand_tiles(mask):
    return jnp.repeat(jnp.repeat(mask, TILE, 0), TILE, 1)


def local(l_panels, u_panels, l_masks, u_masks, ancestor_tiles, initial):
    col_index = lax.axis_index("col")
    depth_cols = l_panels.shape[2]
    width_cols = u_panels.shape[2]
    row_count = initial.shape[0]
    lmask_mine = lax.dynamic_slice_in_dim(
        l_masks[0], col_index * (depth_cols // TILE), depth_cols // TILE, 1
    )
    lpanel = l_panels[0] * expand_tiles(lmask_mine).astype(jnp.bfloat16)
    umask_mine = lax.dynamic_slice_in_dim(
        u_masks[0], col_index * (width_cols // TILE), width_cols // TILE, 1
    )
    upanel = u_panels[0] * expand_tiles(umask_mine).astype(jnp.bfloat16)
    full_panel = lax.all_gather(lpanel, "col", axis=1, tiled=True)
    product = jnp.dot(full_panel, upanel, preferred_element_type=jnp.float32)
    summed = lax.psum_scatter(product, "layer", scatter_dimension=0, tiled=True)
    row_ids = lax.axis_index("layer") * row_count + jnp.arange(row_count, dtype=jnp.int32)
    tile_ids = jnp.arange(ancestor_tiles.shape[0], dtype=jnp.int32)
    onehot = (row_ids[:, None] // TILE == tile_ids[None, :]).astype(jnp.float32)
    row_pattern = jnp.dot(
        onehot, ancestor_tiles.astype(jnp.float32), preferred_element_type=jnp.float32
    )
    col_pattern = lax.dynamic_slice_in_dim(
        row_pattern, col_index * (width_cols // TILE), width_cols // TILE, 1
    )
    pattern = jnp.repeat(col_pattern, TILE, 1)
    return initial - pattern * summed


def solution(mesh):
    return jax.shard_map(
        local,
        mesh=mesh,
        in_specs=(
            P("layer", None, "col"),
            P("layer", None, "col"),
            P("layer", None, None),
            P("layer", None, None),
            P(),
            P("layer", "col"),
        ),
        out_specs=P("layer", "col"),
        check_vma=False,
    )
```

profile of v0, /device:TPU:8, one launch (start us, length us, event | category | flops | bytes accessed | tf_op | source)
XLA Modules:
  0.0 265.6 jit_solution(10379563578866441089)
XLA Ops:
  6.5 0.0 all-gather.2.cloned.1.call-start
  6.5 0.8 fusion.4
  7.3 0.1 broadcast_in_dim.18
  7.4 2.5 broadcast_in_dim.19
  9.9 0.0 copy-start
  9.9 0.5 copy.15
  10.4 1.1 copy-done
  11.5 1.6 bitcast_multiply_fusion.2
  13.0 0.0 all-gather.2.cloned.1.call-update
  13.1 0.0 reduce-scatter.2.cloned.1.call-start
  13.1 0.1 broadcast_in_dim.20
  13.2 2.5 broadcast_in_dim.21
  15.7 0.5 copy.16
  16.2 85.6 %all-gather.2.cloned.1.call-done = bf16[2048,2048]{1,0:T(8,128)(2,1)} async-done(((bf16[2048,512]{1,0:T(8,128)(2,1)}), bf16[2048,2048]{1,0:T(8,128)(2,1)}) %all-gather.2.cloned.1.call-update) | async-done | bytes 8388624 | tf_op jit(solution)/shard_map/all_gather | solution.py:26
  101.8 10.5 %fusion = f32[2048,512]{1,0:T(8,128)} fusion(bf16[2048,2048]{1,0:T(8,128)(2,1)} %all-gather.2.cloned.1.call-done, bf16[2048,512]{1,0:T(8,128)(2,1)S(1)} %bitcast.23, bf16[1,2048,512]{2,1,0:T(8,128)(2,1)} %param.7), kind=kOutput, calls=%fused_computation.1 | convolution fusion | flops 4296015872 | bytes 16777216 | tf_op jit(solution)/shard_map/dot_general | solution.py:27
  112.2 0.0 copy-start.2
  112.2 0.0 copy-start.1
  112.2 0.0 reduce-scatter.2.cloned.1.call-update
  112.3 0.6 copy-done.2
  112.9 0.2 fusion.1
  113.1 0.1 copy.7
  113.2 0.1 broadcast_in_dim.17
  113.3 143.9 %reduce-scatter.2.cloned.1.call-done = f32[32,512]{1,0:T(8,128)} async-done(((f32[2048,512]{1,0:T(8,128)}), f32[32,512]{1,0:T(8,128)}) %reduce-scatter.2.cloned.1.call-update) | async-done | bytes 65552 | tf_op jit(solution)/shard_map/reduce_scatter | solution.py:28
  257.2 0.0 copy-done.1
  257.2 1.5 multiply_subtract_fusion
  (3 shorter events, 0.0 us)
Async XLA Ops:
  6.5 95.2 %all-gather.2.cloned.1.call-start = ((), (), s32[]{:S(2)}) async-start(), calls=%async_computation.1 | async-start | bytes 10485760 | tf_op jit(solution)/shard_map/all_gather | solution.py:26
  9.9 1.6 copy-start
  13.1 244.2 %reduce-scatter.2.cloned.1.call-start = ((), (), s32[]{:S(2)}) async-start(), calls=%async_computation.2 | async-start | bytes 4259840 | tf_op jit(solution)/shard_map/reduce_scatter | solution.py:28
  112.2 0.7 copy-start.2
  112.2 145.0 %copy-start.1 = (f32[32,512]{1,0:T(8,128)S(1)}, f32[32,512]{1,0:T(8,128)}, u32[]{:S(2)}) copy-start(f32[32,512]{1,0:T(8,128)} %param.11) | copy-start | bytes 196612
Sparse Core Ops, SparseCore 0:
  13.2 88.5 all-gather.1
  112.4 144.8 reduce-scatter.1
where the time goes:
time: 266 us
  waiting for transfers between devices  230 us (86%)
  between operations  13.5 us (5%)
  matrix products  10.6 us (4%)
  local copies, waits for them, and re-layouts  8.05 us (3%)
  other arithmetic  3.83 us (1%)
    reduce_scatter x1, waiting for transfers between devices, local(): summed = lax.psum_scatter(product, 'layer', scatter_dimension=0, tiled=True)  144 us
    all_gather x1, waiting for transfers between devices, local(): full_panel = lax.all_gather(lpanel, 'col', axis=1, tiled=True)  85.6 us
    dot_general x1, matrix products, local(): product = jnp.dot(full_panel, upanel, preferred_element_type=jnp.float32)  10.5 us
  transfers between devices with their start and end apart: 2, of which 2 were waited for; matrix products, arithmetic and copies ran while one was open for 1% of the time, Pallas kernels for 0%

commit v1 on v0

--- a/solution.py
+++ b/solution.py
@@ -23,7 +23,12 @@
         u_masks[0], col_index * (width_cols // TILE), width_cols // TILE, 1
     )
     upanel = u_panels[0] * expand_tiles(umask_mine).astype(jnp.bfloat16)
-    full_panel = lax.all_gather(lpanel, "col", axis=1, tiled=True)
+    ring = [lpanel]
+    for hop in range(3):
+        ring.append(lax.ppermute(ring[-1], "col", [(dev, (dev + 1) % 4) for dev in range(4)]))
+    full_panel = jnp.roll(
+        jnp.concatenate(ring[::-1], axis=1), (lax.axis_index("col") + 1) * ring[0].shape[1], axis=1
+    )
     product = jnp.dot(full_panel, upanel, preferred_element_type=jnp.float32)
     summed = lax.psum_scatter(product, "layer", scatter_dimension=0, tiled=True)
     row_ids = lax.axis_index("layer") * row_count + jnp.arange(row_count, dtype=jnp.int32)

time: 266 us -> 325 us (1.22)
  waiting for transfers between devices: 230 us -> 278 us
  local copies, waits for them, and re-layouts: 8.05 us -> 19.7 us
  starting transfers between devices: 0.04 us -> 5 us
  matrix products: 10.6 us -> 6.18 us
    ppermute x0 -> x3, waiting for transfers between devices: none -> 130 us  [local(): lax.ppermute(ring[-1], 'col', [(dev, (dev + 1) % 4) for dev in range(4)])]
    all_gather x1 -> x0, waiting for transfers between devices: 85.6 us -> none  [local(): full_panel = lax.all_gather(lpanel, 'col', axis=1, tiled=True)]
    unnamed x9 -> x24, local copies, waits for them, and re-layouts: 2.76 us -> 14.2 us
    ppermute x0 -> x3, starting transfers between devices: none -> 5 us  [local(): lax.ppermute(ring[-1], 'col', [(dev, (dev + 1) % 4) for dev in range(4)])]
    dot_general x1, matrix products: 10.5 us -> 6 us  [local(): product = jnp.dot(full_panel, upanel, preferred_element_type=jnp.float32)]
    reduce_scatter x1, waiting for transfers between devices: 144 us -> 147 us  [local(): summed = lax.psum_scatter(product, 'layer', scatter_dimension=0, tiled=True)]
  transfers between devices with their start and end apart: 2 -> 4, of which waited for: 2 -> 4; matrix products, arithmetic and copies ran while one was open for 1% -> 1% of each run, Pallas kernels for 0% -> 0%
where the time goes in v1:
time: 325 us
  waiting for transfers between devices  278 us (86%)
  local copies, waits for them, and re-layouts  19.7 us (6%)
  between operations  13.6 us (4%)
  matrix products  6.18 us (2%)
  starting transfers between devices  5 us (2%)
    reduce_scatter x1, waiting for transfers between devices, local(): summed = lax.psum_scatter(product, 'layer', scatter_dimension=0, tiled=True)  147 us
    ppermute x3, waiting for transfers between devices, local(): lax.ppermute(ring[-1], 'col', [(dev, (dev + 1) % 4) for dev in range(4)])  130 us
    unnamed x24, local copies, waits for them, and re-layouts  14.2 us
  transfers between devices with their start and end apart: 4, of which 4 were waited for; matrix products, arithmetic and copies ran while one was open for 1% of the time, Pallas kernels for 0%

profile of v1, /device:TPU:8, one launch (start us, length us, event | category | flops | bytes accessed | tf_op | source)
XLA Modules:
  0.0 324.8 jit_solution(15249284741292936938)
XLA Ops:
  6.5 0.9 fusion.5
  7.5 0.1 broadcast_in_dim.18
  7.5 2.5 broadcast_in_dim.19
  10.0 0.5 copy.15
  10.6 0.2 bitcast_multiply_fusion.2
  10.8 1.7 collective-permute-start
  12.4 45.8 %collective-permute-done = bf16[2048,512]{1,0:T(8,128)(2,1)S(1)} collective-permute-done((bf16[2048,512]{1,0:T(8,128)(2,1)S(1)}, bf16[2048,512]{1,0:T(8,128)(2,1)S(1)}, u32[]{:S(2)}, u32[]{:S(2)}) %collective-permute-start) | collective-permute-done | bytes 2097184 | tf_op jit(solution)/shard_map/ppermute | solution.py:28
  58.2 1.3 copy-done
  59.5 1.6 collective-permute-start.1
  61.1 44.8 %collective-permute-done.1 = bf16[2048,512]{1,0:T(8,128)(2,1)} collective-permute-done((bf16[2048,512]{1,0:T(8,128)(2,1)S(1)}, bf16[2048,512]{1,0:T(8,128)(2,1)}, u32[]{:S(2)}, u32[]{:S(2)}) %collective-permute-start.1) | collective-permute-done | bytes 2097184 | tf_op jit(solution)/shard_map/ppermute | solution.py:28
  106.0 1.8 collective-permute-start.2
  107.7 0.1 broadcast_in_dim.20
  107.8 2.5 broadcast_in_dim.21
  110.3 1.8 copy.16
  112.1 39.5 %collective-permute-done.2 = bf16[2048,512]{1,0:T(8,128)(2,1)} collective-permute-done((bf16[2048,512]{1,0:T(8,128)(2,1)}, bf16[2048,512]{1,0:T(8,128)(2,1)}, u32[]{:S(2)}, u32[]{:S(2)}) %collective-permute-start.2) | collective-permute-done | bytes 2097184 | tf_op jit(solution)/shard_map/ppermute | solution.py:28
  151.7 1.8 constant_dynamic-update-slice_fusion.7
  153.5 1.8 constant_dynamic-update-slice_fusion.6
  155.4 0.3 constant_dynamic-update-slice_fusion.5
  155.6 0.3 constant_dynamic-update-slice_fusion.4
  155.9 1.9 constant_dynamic-update-slice_fusion.3
  157.8 1.8 constant_dynamic-update-slice_fusion.2
  159.6 0.3 constant_dynamic-update-slice_fusion.1
  159.9 0.3 constant_dynamic-update-slice_fusion
  160.2 1.0 copy-done.3
  161.2 0.6 copy-done.5
  161.9 6.0 %fusion = f32[2048,512]{1,0:T(8,128)} fusion(bf16[2048,4096]{1,0:T(8,128)(2,1)S(1)} %constant_dynamic-update-slice_fusion, s32[]{:T(128)S(6)} %select_n.31, bf16[2048,512]{1,0:T(8,128)(2,1)S(1)} %bitcast.22, bf16[1,2048,512]{2,1,0:T(8,128)(2,1)S(1)} %copy-done.5), kind=kOutput, calls=%fused_computation | convolution fusion | flops 4296015872 | bytes 16777220 | tf_op jit(solution)/shard_map/dot_general | solution.py:32
  167.9 0.6 copy-done.6
  168.5 0.2 fusion.2
  168.7 0.1 copy.7
  168.8 0.1 broadcast_in_dim.17
  169.0 147.5 %reduce-scatter.2.cloned.1.call-done = f32[32,512]{1,0:T(8,128)} async-done(((f32[2048,512]{1,0:T(8,128)}), f32[32,512]{1,0:T(8,128)}) %reduce-scatter.2.cloned.1.call-update) | async-done | bytes 65552 | tf_op jit(solution)/shard_map/reduce_scatter | solution.py:33
  316.4 1.5 multiply_subtract_fusion
  (15 shorter events, 0.1 us)
Async XLA Ops:
  6.5 309.9 %reduce-scatter.2.cloned.1.call-start = ((), (), s32[]{:S(2)}) async-start(), calls=%async_computation.1 | async-start | bytes 4259840 | tf_op jit(solution)/shard_map/reduce_scatter | solution.py:33
  6.5 4.0 %copy-start.2 = (bf16[1,2048,512]{2,1,0:T(8,128)(2,1)S(1)}, bf16[1,2048,512]{2,1,0:T(8,128)(2,1)}, u32[]{:S(2)}) copy-start(bf16[1,2048,512]{2,1,0:T(8,128)(2,1)} %param.6) | copy-start | bytes 6291460
  10.8 47.4 %collective-permute-start = (bf16[2048,512]{1,0:T(8,128)(2,1)S(1)}, bf16[2048,512]{1,0:T(8,128)(2,1)S(1)}, u32[]{:S(2)}, u32[]{:S(2)}) collective-permute-start(bf16[2048,512]{1,0:T(8,128)(2,1)S(1)} %bitcast_multiply_fusion.2), channel_id=1, source_target_pairs={{0,1},{1,2},{2,3},{3,0},{4,5},{5,6},{6,7},{7,4},{8,9},{9,10},{10,1... | collective-permute-start | bytes 6291464 | tf_op jit(solution)/shard_map/ppermute | solution.py:28
  58.2 1.3 copy-start
  59.5 46.4 %collective-permute-start.1 = (bf16[2048,512]{1,0:T(8,128)(2,1)S(1)}, bf16[2048,512]{1,0:T(8,128)(2,1)}, u32[]{:S(2)}, u32[]{:S(2)}) collective-permute-start(bf16[2048,512]{1,0:T(8,128)(2,1)S(1)} %collective-permute-done), channel_id=1, source_target_pairs={{0,1},{1,2},{2,3},{3,0},{4,5},{5,6},{6,7},{7,4},{8,9},{9,10},{10,1... | collective-permute-start | bytes 6291464 | tf_op jit(solution)/shard_map/ppermute | solution.py:28
  106.0 45.7 %collective-permute-start.2 = (bf16[2048,512]{1,0:T(8,128)(2,1)}, bf16[2048,512]{1,0:T(8,128)(2,1)}, u32[]{:S(2)}, u32[]{:S(2)}) collective-permute-start(bf16[2048,512]{1,0:T(8,128)(2,1)} %collective-permute-done.1), channel_id=1, source_target_pairs={{0,1},{1,2},{2,3},{3,0},{4,5},{5,6},{6,7},{7,4},{8,9},{9,10},{10,1... | collective-permute-start | bytes 6291464 | tf_op jit(solution)/shard_map/ppermute | solution.py:28
  112.1 43.2 %copy-start.1 = (bf16[2048,512]{1,0:T(8,128)(2,1)S(1)}, bf16[2048,512]{1,0:T(8,128)(2,1)}, u32[]{:S(2)}) copy-start(bf16[2048,512]{1,0:T(8,128)(2,1)} %copy-done) | copy-start | bytes 6291460
  159.6 1.6 copy-start.3
  159.6 2.2 copy-start.5
  167.8 0.7 copy-start.6
  167.9 148.6 %copy-start.4 = (f32[32,512]{1,0:T(8,128)S(1)}, f32[32,512]{1,0:T(8,128)}, u32[]{:S(2)}) copy-start(f32[32,512]{1,0:T(8,128)} %param.11) | copy-start | bytes 196612
Sparse Core Ops, SparseCore 0:
  168.0 148.3 reduce-scatter.1
